TPU v7x, 32 devices: a whole 2x2x4 slice. The times are simulated.
32 devices in a mesh: gx: 4 (over z), yz: 8 (over y, x, core).
Axes of the slice: x: 2, y: 2, z: 4, core: 2. Of those that a mesh axis runs over, the one named last changes fastest.
Arguments:
- features: bfloat16 [384, 96, 512], P(('gx', 'yz')), may hold values from -6 to 6
- occupancy: int32 [384, 512], P(('gx', 'yz')), may hold values 0 or 1
- neighbours: int32 [384, 27], P(('gx', 'yz')), may hold values from 0 to 84, as said below
- exports: int32 [256], P(('gx', 'yz')), may hold values from 0 to 11, as said below
- coarse_map: int32 [384, 2], P(('gx', 'yz')), may hold values from 0 to 7, as said below
- owners: int32 [128], P(('gx', 'yz')), may hold values from 0 to 7, as said below
- w_sub: bfloat16 [27, 96, 96], replicated, may hold values from -0.15625 to 0.15625
- w_down: bfloat16 [8, 192, 96], replicated, may hold values from -0.3125 to 0.3125
- cotangent: bfloat16 [256, 192, 512], P(('gx', 'yz')), may hold values from -6 to 6
Outputs:
- coarse: bfloat16 [256, 192, 512], P(('gx', 'yz'))
- grad_features: bfloat16 [384, 96, 512], P(('gx', 'yz'))
- grad_sub: float32 [27, 96, 96], replicated
- grad_down: float32 [8, 192, 96], replicated
Inputs may be any that keep to these rules, and one draw needn't show every extreme that they name: `neighbours`: entry 13 of a brick is its own slot. Entries follow the geometry of a map of 8-voxel bricks in which device (i, j) holds a region of 4 x 4 x 2 brick cells beside the regions of (i +- 1, j +- 1); a brick met at offset k meets the first at the opposite offset. Entries that point to another device name only bricks on that device's side faces. `exports`: each device's 8 entries are distinct slots of its bricks that lie on its region's side faces, and every such brick is listed. `coarse_map`: column 0 is the coarse cell (0 to 3), column 1 the octant; every coarse cell of every device holds exactly 3 of its fine bricks, in distinct octants. The 4 coarse cells of one device have distinct owners; in every gx slab one owner is named by every device of the slab.
All inputs are finite; a program needn't handle non-finite values. No bound on the sum of `occupancy` on one device may be relied on, other than what follows from the above.
Results may differ from a plain program's by a relative error of at most 0.0062.
Values may be sent and summed in bfloat16 or wider, within the bound.
A program may use at most 320 MiB of HBM per device.

v0:
```python
import jax
import jax.numpy as jnp
from jax import lax
from jax.sharding import PartitionSpec as P

EDGE = 8


def padded_2(x, sides, width):
    for axis, dim in sides:
        size, length = (lax.axis_size(axis), x.shape[dim])
        up = [(i, (i + 1) % size) for i in range(size - 1)]
        down = [(j, i) for i, j in up]
        last = lax.slice_in_dim(x, length - width, length, axis=dim)
        initial = lax.slice_in_dim(x, 0, width, axis=dim)
        before = lax.ppermute(last, axis, up)
        after = lax.ppermute(initial, axis, down)
        x = jnp.concatenate([before, x, after], axis=dim)
    return x


def silu_slope(values):
    sig = jax.nn.sigmoid(values)
    return sig * (1.0 + values * (1.0 - sig))


def layer_span(shift, cube_edge):
    if shift < 0:
        return (slice(cube_edge - 1, cube_edge), slice(0, 1))
    if shift > 0:
        return (slice(0, 1), slice(cube_edge + 1, cube_edge + 2))
    return (slice(0, cube_edge), slice(1, cube_edge + 1))


def pad_bricks(lookup, neighbour_ids, cube_edge):
    channels = lookup.shape[1]
    blocks = lookup.reshape(lookup.shape[0], channels, cube_edge, cube_edge, cube_edge)
    padded = jnp.zeros(
        (neighbour_ids.shape[0], channels, cube_edge + 2, cube_edge + 2, cube_edge + 2),
        lookup.dtype,
    )
    for offset in range(27):
        spans = [
            layer_span(shift, cube_edge)
            for shift in (offset // 9 - 1, offset // 3 % 3 - 1, offset % 3 - 1)
        ]
        facing = blocks[:, :, spans[0][0], spans[1][0], spans[2][0]]
        picked = jnp.take(facing, neighbour_ids[:, offset], axis=0)
        padded = padded.at[:, :, spans[0][1], spans[1][1], spans[2][1]].set(picked)
    return padded


def conv_forward(padded, weights, cube_edge):
    result = None
    for offset in range(27):
        start_x, start_y, start_z = (offset // 9, offset // 3 % 3, offset % 3)
        window = padded[
            :,
            :,
            start_x : start_x + cube_edge,
            start_y : start_y + cube_edge,
            start_z : start_z + cube_edge,
        ]
        term = jnp.einsum(
            "oi,bixyz->boxyz", weights[offset], window, preferred_element_type=jnp.float32
        )
        result = term if result is None else result + term
    return result


def conv_transpose(padded, weights, cube_edge):
    result = None
    for offset in range(27):
        start_x, start_y, start_z = (2 - offset // 9, 2 - offset // 3 % 3, 2 - offset % 3)
        window = padded[
            :,
            :,
            start_x : start_x + cube_edge,
            start_y : start_y + cube_edge,
            start_z : start_z + cube_edge,
        ]
        term = jnp.einsum(
            "oi,boxyz->bixyz", weights[offset], window, preferred_element_type=jnp.float32
        )
        result = term if result is None else result + term
    return result


def conv_weights(padded, grads, cube_edge):
    terms = []
    for offset in range(27):
        start_x, start_y, start_z = (offset // 9, offset // 3 % 3, offset % 3)
        window = padded[
            :,
            :,
            start_x : start_x + cube_edge,
            start_y : start_y + cube_edge,
            start_z : start_z + cube_edge,
        ]
        terms.append(
            jnp.einsum("boxyz,bixyz->oi", grads, window, preferred_element_type=jnp.float32)
        )
    return jnp.stack(terms)


def split_fine(values, half_edge):
    rows, channels = (values.shape[0], values.shape[1])
    shaped = values.reshape(rows, channels, half_edge, 2, half_edge, 2, half_edge, 2)
    return shaped.transpose(0, 1, 3, 5, 7, 2, 4, 6).reshape(rows, channels, 8, half_edge**3)


def join_fine(values, half_edge):
    rows, channels = (values.shape[0], values.shape[1])
    shaped = values.reshape(rows, channels, 2, 2, 2, half_edge, half_edge, half_edge)
    return shaped.transpose(0, 1, 5, 2, 6, 3, 7, 4).reshape(rows, channels, 8 * half_edge**3)


def split_block(values, half_edge):
    rows, channels = (values.shape[0], values.shape[1])
    shaped = values.reshape(rows, channels, 2, half_edge, 2, half_edge, 2, half_edge)
    return shaped.transpose(0, 1, 2, 4, 6, 3, 5, 7).reshape(rows, channels, 8, half_edge**3)


def join_block(values, half_edge):
    rows, channels = (values.shape[0], values.shape[1])
    shaped = values.reshape(rows, channels, 2, 2, 2, half_edge, half_edge, half_edge)
    return shaped.transpose(0, 1, 2, 5, 3, 6, 4, 7).reshape(rows, channels, 8 * half_edge**3)


def rim_lookup(own_bricks, exports, forward):
    voxels = own_bricks.shape[2]
    outgoing = jnp.take(own_bricks, exports, axis=0)
    if forward:
        arrived = padded_2(outgoing[None, None], (("gx", 0), ("yz", 1)), 1)
    else:
        arrived = padded_2(outgoing[None, None], (("gx", 0), ("yz", 1)), 1)
    arrived = arrived.reshape(-1, own_bricks.shape[1], voxels)
    blank = jnp.zeros((1, own_bricks.shape[1], voxels), own_bricks.dtype)
    return jnp.concatenate([own_bricks, arrived, blank], axis=0)


def activate_coarse(coarse_pre, cotangent):
    coarse_wide = coarse_pre.astype(jnp.float32)
    grad_coarse = (cotangent.astype(jnp.float32) * silu_slope(coarse_wide)).astype(jnp.bfloat16)
    return grad_coarse


def on_device(
    features, occupancy, neighbours, exports, coarse_map, owners, w_sub, w_down, cotangent
):
    bricks = features.shape[0]
    channels = features.shape[1]
    voxels = features.shape[2]
    half_edge = EDGE // 2
    groups = lax.axis_size("yz")
    live = occupancy.astype(jnp.float32).reshape(bricks, 1, EDGE, EDGE, EDGE)
    masked = features * occupancy.astype(jnp.bfloat16)[:, None, :]
    padded_input = pad_bricks(rim_lookup(masked, exports, True), neighbours, EDGE)
    pre_sub = conv_forward(padded_input, w_sub, EDGE) * live
    hidden = jax.nn.silu(pre_sub).astype(jnp.bfloat16)
    strided = split_fine(hidden.reshape(bricks, channels, voxels), half_edge)
    piece = jnp.einsum("toi,bitu->bou", w_down, strided, preferred_element_type=jnp.float32).astype(
        jnp.bfloat16
    )
    cell_of = coarse_map[:, 0]
    octant_of = coarse_map[:, 1]
    owner_of = jnp.take(owners, cell_of)
    group_ids = jnp.arange(groups, dtype=jnp.int32)
    octant_ids = jnp.arange(8, dtype=jnp.int32)
    select = (
        (owner_of[None, None, :] == group_ids[:, None, None])
        & (octant_of[None, None, :] == octant_ids[None, :, None])
    ).astype(jnp.bfloat16)
    outgoing = join_block(
        jnp.einsum("gob,bcu->gcou", select, piece, preferred_element_type=jnp.float32).astype(
            jnp.bfloat16
        ),
        half_edge,
    )
    coarse_pre = lax.all_to_all(outgoing, "yz", split_axis=0, concat_axis=0, tiled=True)
    grad_coarse = activate_coarse(coarse_pre, cotangent)
    returned = split_block(
        lax.all_to_all(grad_coarse, "yz", split_axis=0, concat_axis=0, tiled=True), half_edge
    )
    grad_piece = jnp.einsum(
        "gob,gcou->bcu", select, returned, preferred_element_type=jnp.float32
    ).astype(jnp.bfloat16)
    coarse = jax.nn.silu(coarse_pre.astype(jnp.float32)).astype(jnp.bfloat16)
    down_local = jnp.einsum(
        "bou,bitu->toi", grad_piece, strided, preferred_element_type=jnp.float32
    )
    grad_hidden = join_fine(
        jnp.einsum("toi,bou->bitu", w_down, grad_piece, preferred_element_type=jnp.float32),
        half_edge,
    )
    grad_hidden = grad_hidden.reshape(bricks, channels, EDGE, EDGE, EDGE)
    grad_pre = (grad_hidden * silu_slope(pre_sub) * live).astype(jnp.bfloat16)
    padded_grad = pad_bricks(
        rim_lookup(grad_pre.reshape(bricks, channels, voxels), exports, False), neighbours, EDGE
    )
    grad_input = conv_transpose(padded_grad, w_sub, EDGE) * live
    grad_features = grad_input.reshape(bricks, channels, voxels).astype(jnp.bfloat16)
    sub_local = conv_weights(padded_input, grad_pre, EDGE)
    grad_sub, grad_down = lax.psum((sub_local, down_local), ("gx", "yz"))
    return (coarse, grad_features, grad_sub, grad_down)


def solution(mesh):
    in_specs = (
        P(("gx", "yz"), None, None),
        P(("gx", "yz"), None),
        P(("gx", "yz"), None),
        P(("gx", "yz")),
        P(("gx", "yz"), None),
        P(("gx", "yz")),
        P(),
        P(),
        P(("gx", "yz"), None, None),
    )
    out_specs = (P(("gx", "yz"), None, None), P(("gx", "yz"), None, None), P(), P())
    return jax.shard_map(
        on_device, mesh=mesh, in_specs=in_specs, out_specs=out_specs, check_vma=False
    )
```

profile of v0, /device:TPU:0, one launch (start us, length us, event | category | flops | bytes accessed | tf_op | source)
XLA Modules:
  0.0 806.1 jit_solution(12787594770374967149)
XLA Ops:
  13.5 6.5 collective-permute-start
  38.3 3.1 pad_maximum_fusion.2
  42.7 4.5 collective-permute-start.2
  47.9 3.3 copy.305
  66.5 6.2 pad_maximum_fusion
  72.7 12.1 %copy.306 = bf16[3,3,8,96,512]{3,2,1,0,4:T(8,128)(2,1)} copy(bf16[3,3,8,96,512]{4,3,2,1,0:T(8,128)(2,1)} %pad_maximum_fusion) | data formatting | bytes 14155776 | tf_op jit(solution)/shard_map/concatenate | solution.py:18
  84.8 8.6 %maximum_maximum_fusion = bf16[85,96,8,8,8]{1,0,4,3,2:T(8,128)(2,1)S(1)} fusion(bf16[72,96,8,8,8]{1,0,4,3,2:T(8,128)(2,1)} %bitcast.1018, bf16[12,96,8,8,8]{1,0,4,3,2:T(8,128)(2,1)S(1)} %bitcast.1024, bf16[85]{0:T(256)(128)(2,1)S(1)} %copy-done.96), kind=kLoop, calls=%fused_computation.57 | loop fusion | flops 25067520 | bytes 16613546 | tf_op jit(solution)/shard_map/concatenate | solution.py:139
  95.0 6.4 copy.325
  113.5 2.7 scatter.180
  144.0 5.1 gather_fusion.15
  170.6 4.2 fusion.66
  184.3 4.5 fusion.281
  191.4 2.7 fusion.289
  194.2 2.8 fusion.293
  202.3 2.7 fusion.305
  205.1 2.8 fusion.309
  207.9 3.1 fusion.313
  211.0 2.8 fusion.317
  216.5 2.8 fusion.325
  221.9 2.8 fusion.333
  227.3 2.8 fusion.341
  232.8 2.7 fusion.349
  235.5 2.7 fusion.353
  238.2 2.8 fusion.357
  243.8 2.7 fusion.365
  246.5 2.7 fusion.369
  249.2 2.8 fusion.373
  257.4 37.2 %multiply_convert_fusion.1 = (bf16[12,96,8,8,8]{1,0,4,3,2:T(8,128)(2,1)S(1)}, f32[12,96,8,8,8]{1,0,4,3,2:T(8,128)}) fusion(f32[12,8,8,8]{0,3,2,1:T(8,128)S(1)} %bitcast.1029, bf16[12,96,10,10,10]{1,0,4,3,2:T(8,128)(2,1)} %constant_dynamic-update-slice_fusion.7, bf16[27,96,96]{2,1,0:T(8,128)(2,1)} %param.141, f32[12,8,8,8,96]{4,0,3,2,1:T(8,128)} %fusion.281, ...), kind=kOutput, calls=%fused_computation.88 | convolution fusion | flops 132120576 | bytes 116736000 | tf_op jit(solution)/shard_map/oi,bixyz->boxyz/dot_general | solution.py:64
  302.5 2.8 copy.349
  305.3 55.4 %all_to_all.10 = bf16[8,192,512]{2,1,0:T(8,128)(2,1)S(1)} all-to-all(bf16[8,192,512]{2,1,0:T(8,128)(2,1)} %copy.349), channel_id=1, replica_groups=mesh['gx'=4,'yz'=8] {'yz'}, dimensions={0} | all-to-all | bytes 3145728 | tf_op jit(solution)/shard_map/all_to_all | solution.py:180
  360.7 3.2 fusion.10
  363.9 4.3 all-to-all-start.1
  368.2 4.2 copy.395
  372.4 16.8 %all-to-all-done.1 = bf16[8,192,512]{2,1,0:T(8,128)(2,1)} async-done(((bf16[8,192,512]{2,1,0:T(8,128)(2,1)}), bf16[8,192,512]{2,1,0:T(8,128)(2,1)}, u32[]{:S(2)}, u32[]{:S(2)}) %all-to-all-start.1) | async-done | bytes 1572896 | tf_op jit(solution)/shard_map/all_to_all | solution.py:183
  389.2 3.2 copy.350
  392.4 3.5 copy.351
  396.0 3.6 reshape.2536
  407.3 2.9 gather_fusion.29
  413.1 5.0 collective-permute-start.4
  418.1 3.0 fusion.72
  456.2 4.5 collective-permute-start.6
  466.5 132.7 %all-reduce.5.cloned.1.call-done = (f32[27,96,96]{2,1,0:T(8,128)}, f32[8,192,96]{1,0,2:T(8,128)}) async-done(((f32[27,96,96]{2,1,0:T(8,128)}, f32[8,192,96]{1,0,2:T(8,128)}), (f32[27,96,96]{2,1,0:T(8,128)}, f32[8,192,96]{1,0,2:T(8,128)})) %all-reduce.5.cloned.1.call-update) | async-done | bytes 1585168 | tf_op jit(solution)/shard_map/psum | solution.py:204
  601.5 6.2 pad_maximum_fusion.1
  607.8 12.1 %copy.460 = bf16[3,3,8,96,512]{3,2,1,0,4:T(8,128)(2,1)} copy(bf16[3,3,8,96,512]{4,3,2,1,0:T(8,128)(2,1)} %pad_maximum_fusion.1) | data formatting | bytes 14155776 | tf_op jit(solution)/shard_map/concatenate | solution.py:139
  619.8 8.6 %maximum_maximum_fusion.1 = bf16[85,96,8,8,8]{1,0,4,3,2:T(8,128)(2,1)S(1)} fusion(bf16[72,96,8,8,8]{1,0,4,3,2:T(8,128)(2,1)} %bitcast.1017, bf16[12,96,8,8,8]{1,0,4,3,2:T(8,128)(2,1)S(1)} %multiply_convert_fusion, bf16[85]{0:T(256)(128)(2,1)S(1)} %copy-done.97), kind=kLoop, calls=%fused_computation.58 | loop fusion | flops 25067520 | bytes 16613546 | tf_op jit(solution)/shard_map/concatenate | solution.py:139
  634.5 6.3 copy.375
  666.3 5.1 gather_fusion.43
  671.5 2.8 copy.381
  676.4 2.8 copy.369
  687.4 3.1 fusion.279
  690.5 2.7 fusion.283
  693.2 2.8 fusion.287
  701.3 2.7 fusion.299
  704.0 2.8 fusion.303
  709.4 3.0 fusion.311
  715.2 2.8 fusion.319
  720.6 2.7 fusion.327
  726.0 2.8 fusion.335
  731.4 2.7 fusion.343
  736.8 2.8 fusion.351
  742.3 2.7 fusion.359
  745.0 2.7 fusion.363
  747.7 2.8 fusion.367
  758.6 35.2 %fusion.1 = bf16[12,96,8,8,8]{1,0,4,3,2:T(8,128)(2,1)S(1)} fusion(f32[12,8,8,8,96]{4,0,3,2,1:T(8,128)} %fusion.279, f32[12,8,8,8,96]{4,0,3,2,1:T(8,128)} %fusion.283, f32[12,8,8,8,96]{4,0,3,2,1:T(8,128)} %fusion.287, f32[12,8,8,8,96]{4,0,3,2,1:T(8,128)} %fusion.291, f32[12,8,8,8,96]{4,0,3,2,1:T(8,128)} %fusion.295, f32[12,8,8,8,96]{4,0,3,2,1:T(8,128)} %fusion.299, ...), kind=kOutput, calls=%fused_computation.66 | convolution fusion | flops 129761280 | bytes 114376704 | tf_op jit(solution)/shard_map/oi,boxyz->bixyz/dot_general | solution.py:82
  (507 shorter events, 280.5 us)
Async XLA Ops:
  7.2 289.4 %copy-start = (bf16[8,192,96]{2,1,0:T(8,128)(2,1)S(1)}, bf16[8,192,96]{2,1,0:T(8,128)(2,1)}, u32[]{:S(2)}) copy-start(bf16[8,192,96]{2,1,0:T(8,128)(2,1)} %param.142) | copy-start | bytes 884740
  7.2 12.8 %copy-start.11 = (s32[12,27]{1,0:T(8,128)S(1)}, s32[12,27]{1,0:T(8,128)}, u32[]{:S(2)}) copy-start(s32[12,27]{1,0:T(8,128)} %param.137) | copy-start | bytes 3892
  7.2 13.6 %copy-start.95 = (s32[12,2]{0,1:T(2,128)S(1)}, s32[12,2]{0,1:T(2,128)}, u32[]{:S(2)}) copy-start(s32[12,2]{0,1:T(2,128)} %param.139) | copy-start | bytes 292
  7.2 15.0 %copy-start.5 = (s32[4]{0:T(128)S(1)}, s32[4]{0:T(128)}, u32[]{:S(2)}) copy-start(s32[4]{0:T(128)} %param.140) | copy-start | bytes 52
  7.9 33.5 %copy-start.98 = (pred[8]{0:T(512)(128)(4,1)}, pred[8]{0:T(512)(128)(4,1)S(1)}, u32[]{:S(2)}) copy-start(pred[8]{0:T(512)(128)(4,1)S(1)} %compare_and_fusion.27) | copy-start | bytes 28
  8.6 32.8 %copy-start.33 = (s32[1024]{0:T(1024)}, s32[1024]{0:T(1024)S(1)}, u32[]{:S(2)}) copy-start(s32[1024]{0:T(1024)S(1)} %pad_clamp_fusion.28) | copy-start | bytes 12292
  11.4 30.0 %copy-start.8 = (bf16[12,96,512]{2,1,0:T(8,128)(2,1)}, bf16[12,96,512]{2,1,0:T(8,128)(2,1)S(1)}, u32[]{:S(2)}) copy-start(bf16[12,96,512]{2,1,0:T(8,128)(2,1)S(1)} %broadcast_multiply_fusion) | copy-start | bytes 3538948
  12.2 26.1 %collective-permute-start.1 = (bf16[1,1,8,96,512]{4,3,2,1,0:T(8,128)(2,1)S(1)}, bf16[1,1,8,96,512]{4,3,2,1,0:T(8,128)(2,1)S(1)}, u32[]{:S(2)}, u32[]{:S(2)}) collective-permute-start(bf16[1,1,8,96,512]{4,3,2,1,0:T(8,128)(2,1)S(1)} %select_bitcast_fusion.1), channel_id=1, source_target_pairs={{8,0},{16,8},{24,16},{9,1},{17,9},{25,17},{10,2},{18,10},{26,18},{... | collective-permute-start | bytes 2359304 | tf_op jit(solution)/shard_map/ppermute | solution.py:17
  13.5 24.8 %collective-permute-start = (bf16[1,1,8,96,512]{4,3,2,1,0:T(8,128)(2,1)S(1)}, bf16[1,1,8,96,512]{4,3,2,1,0:T(8,128)(2,1)}, u32[]{:S(2)}, u32[]{:S(2)}) collective-permute-start(bf16[1,1,8,96,512]{4,3,2,1,0:T(8,128)(2,1)S(1)} %select_bitcast_fusion.1), channel_id=1, source_target_pairs={{0,8},{8,16},{16,24},{1,9},{9,17},{17,25},{2,10},{10,18},{18,26},{... | collective-permute-start | bytes 2359304 | tf_op jit(solution)/shard_map/ppermute | solution.py:16
  20.3 26.9 %copy-start.52 = (s32[12]{0:T(128)}, s32[12]{0:T(128)S(1)}, u32[]{:S(2)}) copy-start(s32[12]{0:T(128)S(1)} %get-tuple-element.700) | copy-start | bytes 148
  20.3 26.9 %copy-start.70 = (s32[12]{0:T(128)}, s32[12]{0:T(128)S(1)}, u32[]{:S(2)}) copy-start(s32[12]{0:T(128)S(1)} %get-tuple-element.699) | copy-start | bytes 148
  20.8 9.8 %copy-start.64 = (s32[12]{0:T(128)}, s32[12]{0:T(128)S(1)}, u32[]{:S(2)}) copy-start(s32[12]{0:T(128)S(1)} %get-tuple-element.686) | copy-start | bytes 148
  20.8 26.3 %copy-start.53 = (s32[12]{0:T(128)}, s32[12]{0:T(128)S(1)}, u32[]{:S(2)}) copy-start(s32[12]{0:T(128)S(1)} %get-tuple-element.698) | copy-start | bytes 148
  20.9 26.3 %copy-start.54 = (s32[12]{0:T(128)}, s32[12]{0:T(128)S(1)}, u32[]{:S(2)}) copy-start(s32[12]{0:T(128)S(1)} %get-tuple-element.696) | copy-start | bytes 148
  20.9 26.3 %copy-start.55 = (s32[12]{0:T(128)}, s32[12]{0:T(128)S(1)}, u32[]{:S(2)}) copy-start(s32[12]{0:T(128)S(1)} %get-tuple-element.697) | copy-start | bytes 148
  20.9 26.3 %copy-start.56 = (s32[12]{0:T(128)}, s32[12]{0:T(128)S(1)}, u32[]{:S(2)}) copy-start(s32[12]{0:T(128)S(1)} %get-tuple-element.694) | copy-start | bytes 148
  20.9 26.3 %copy-start.57 = (s32[12]{0:T(128)}, s32[12]{0:T(128)S(1)}, u32[]{:S(2)}) copy-start(s32[12]{0:T(128)S(1)} %get-tuple-element.695) | copy-start | bytes 148
  20.9 26.3 %copy-start.58 = (s32[12]{0:T(128)}, s32[12]{0:T(128)S(1)}, u32[]{:S(2)}) copy-start(s32[12]{0:T(128)S(1)} %get-tuple-element.692) | copy-start | bytes 148
  20.9 26.3 %copy-start.59 = (s32[12]{0:T(128)}, s32[12]{0:T(128)S(1)}, u32[]{:S(2)}) copy-start(s32[12]{0:T(128)S(1)} %get-tuple-element.693) | copy-start | bytes 148
  20.9 26.3 %copy-start.60 = (s32[12]{0:T(128)}, s32[12]{0:T(128)S(1)}, u32[]{:S(2)}) copy-start(s32[12]{0:T(128)S(1)} %get-tuple-element.690) | copy-start | bytes 148
  20.9 26.3 %copy-start.61 = (s32[12]{0:T(128)}, s32[12]{0:T(128)S(1)}, u32[]{:S(2)}) copy-start(s32[12]{0:T(128)S(1)} %get-tuple-element.691) | copy-start | bytes 148
  20.9 26.3 %copy-start.62 = (s32[12]{0:T(128)}, s32[12]{0:T(128)S(1)}, u32[]{:S(2)}) copy-start(s32[12]{0:T(128)S(1)} %get-tuple-element.688) | copy-start | bytes 148
  20.9 26.3 %copy-start.63 = (s32[12]{0:T(128)}, s32[12]{0:T(128)S(1)}, u32[]{:S(2)}) copy-start(s32[12]{0:T(128)S(1)} %get-tuple-element.689) | copy-start | bytes 148
  21.0 26.3 %copy-start.66 = (s32[12]{0:T(128)}, s32[12]{0:T(128)S(1)}, u32[]{:S(2)}) copy-start(s32[12]{0:T(128)S(1)} %get-tuple-element.684) | copy-start | bytes 148
  21.0 26.3 %copy-start.67 = (s32[12]{0:T(128)}, s32[12]{0:T(128)S(1)}, u32[]{:S(2)}) copy-start(s32[12]{0:T(128)S(1)} %get-tuple-element.685) | copy-start | bytes 148
  21.0 26.3 %copy-start.68 = (s32[12]{0:T(128)}, s32[12]{0:T(128)S(1)}, u32[]{:S(2)}) copy-start(s32[12]{0:T(128)S(1)} %get-tuple-element.682) | copy-start | bytes 148
  21.0 26.3 %copy-start.69 = (s32[12]{0:T(128)}, s32[12]{0:T(128)S(1)}, u32[]{:S(2)}) copy-start(s32[12]{0:T(128)S(1)} %get-tuple-element.683) | copy-start | bytes 148
  21.0 26.3 %copy-start.71 = (s32[12]{0:T(128)}, s32[12]{0:T(128)S(1)}, u32[]{:S(2)}) copy-start(s32[12]{0:T(128)S(1)} %get-tuple-element.681) | copy-start | bytes 148
  25.2 87.7 %copy-start.29 = (s32[1024]{0:T(1024)}, s32[1024]{0:T(1024)S(1)}, u32[]{:S(2)}) copy-start(s32[1024]{0:T(1024)S(1)} %pad_clamp_fusion.27) | copy-start | bytes 12292
  30.0 88.1 %copy-start.30 = (s32[1024]{0:T(1024)}, s32[1024]{0:T(1024)S(1)}, u32[]{:S(2)}) copy-start(s32[1024]{0:T(1024)S(1)} %pad_clamp_fusion.9) | copy-start | bytes 12292
  30.0 87.5 %copy-start.31 = (s32[1024]{0:T(1024)}, s32[1024]{0:T(1024)S(1)}, u32[]{:S(2)}) copy-start(s32[1024]{0:T(1024)S(1)} %pad_clamp_fusion.7) | copy-start | bytes 12292
  30.7 86.2 %copy-start.32 = (s32[1024]{0:T(1024)}, s32[1024]{0:T(1024)S(1)}, u32[]{:S(2)}) copy-start(s32[1024]{0:T(1024)S(1)} %pad_clamp_fusion.3) | copy-start | bytes 12292
  41.4 25.0 %collective-permute-start.3 = (bf16[3,1,8,96,512]{4,3,2,1,0:T(8,128)(2,1)}, bf16[3,1,8,96,512]{4,3,2,1,0:T(8,128)(2,1)}, u32[]{:S(2)}, u32[]{:S(2)}) collective-permute-start(bf16[3,1,8,96,512]{4,3,2,1,0:T(8,128)(2,1)} %pad_maximum_fusion.2), channel_id=1, source_target_pairs={{1,0},{2,1},{3,2},{4,3},{5,4},{6,5},{7,6},{9,8},{10,9},{11,10},{12... | collective-permute-start | bytes 7077896 | tf_op jit(solution)/shard_map/ppermute | solution.py:17
  42.7 23.7 %collective-permute-start.2 = (bf16[3,1,8,96,512]{4,3,2,1,0:T(8,128)(2,1)}, bf16[3,1,8,96,512]{4,3,2,1,0:T(8,128)(2,1)}, u32[]{:S(2)}, u32[]{:S(2)}) collective-permute-start(bf16[3,1,8,96,512]{4,3,2,1,0:T(8,128)(2,1)} %pad_maximum_fusion.2), channel_id=1, source_target_pairs={{0,1},{1,2},{2,3},{3,4},{4,5},{5,6},{6,7},{8,9},{9,10},{10,11},{11... | collective-permute-start | bytes 7077896 | tf_op jit(solution)/shard_map/ppermute | solution.py:16
  52.1 350.5 %copy-start.12 = (f32[12,512]{0,1:T(8,128)}, f32[12,512]{0,1:T(8,128)S(1)}, u32[]{:S(2)}) copy-start(f32[12,512]{0,1:T(8,128)S(1)} %copy.457) | copy-start | bytes 73732
  72.7 12.1 %copy-start.96 = (bf16[85]{0:T(256)(128)(2,1)S(1)}, bf16[85]{0:T(256)(128)(2,1)}, u32[]{:S(2)}) copy-start(bf16[85]{0:T(256)(128)(2,1)} %pad.231.clone) | copy-start | bytes 514
  153.3 21.5 %copy-start.88 = (pred[12]{0:T(512)(128)(4,1)S(1)}, pred[12]{0:T(512)(128)(4,1)}, u32[]{:S(2)}) copy-start(pred[12]{0:T(512)(128)(4,1)} %get-tuple-element.810) | copy-start | bytes 40
  153.3 22.3 %copy-start.14 = (bf16[12,96,8]{1,2,0:T(8,128)(2,1)S(1)}, bf16[12,96,8]{1,2,0:T(8,128)(2,1)}, u32[]{:S(2)}) copy-start(bf16[12,96,8]{1,2,0:T(8,128)(2,1)} %gather_fusion.17) | copy-start | bytes 55300
  153.3 22.3 %copy-start.47 = (pred[12]{0:T(512)(128)(4,1)S(1)}, pred[12]{0:T(512)(128)(4,1)}, u32[]{:S(2)}) copy-start(pred[12]{0:T(512)(128)(4,1)} %get-tuple-element.809) | copy-start | bytes 40
  153.3 23.0 %copy-start.86 = (pred[12]{0:T(512)(128)(4,1)S(1)}, pred[12]{0:T(512)(128)(4,1)}, u32[]{:S(2)}) copy-start(pred[12]{0:T(512)(128)(4,1)} %get-tuple-element.808) | copy-start | bytes 40
  153.3 23.9 %copy-start.44 = (pred[12]{0:T(512)(128)(4,1)S(1)}, pred[12]{0:T(512)(128)(4,1)}, u32[]{:S(2)}) copy-start(pred[12]{0:T(512)(128)(4,1)} %get-tuple-element.807) | copy-start | bytes 40
  153.4 24.5 %copy-start.79 = (pred[12]{0:T(512)(128)(4,1)S(1)}, pred[12]{0:T(512)(128)(4,1)}, u32[]{:S(2)}) copy-start(pred[12]{0:T(512)(128)(4,1)} %get-tuple-element.806) | copy-start | bytes 40
  153.4 25.2 %copy-start.41 = (pred[12]{0:T(512)(128)(4,1)S(1)}, pred[12]{0:T(512)(128)(4,1)}, u32[]{:S(2)}) copy-start(pred[12]{0:T(512)(128)(4,1)} %get-tuple-element.805) | copy-start | bytes 40
  153.4 25.9 %copy-start.77 = (pred[12]{0:T(512)(128)(4,1)S(1)}, pred[12]{0:T(512)(128)(4,1)}, u32[]{:S(2)}) copy-start(pred[12]{0:T(512)(128)(4,1)} %get-tuple-element.804) | copy-start | bytes 40
  153.4 26.5 %copy-start.38 = (pred[12]{0:T(512)(128)(4,1)S(1)}, pred[12]{0:T(512)(128)(4,1)}, u32[]{:S(2)}) copy-start(pred[12]{0:T(512)(128)(4,1)} %get-tuple-element.803) | copy-start | bytes 40
  153.4 27.3 %copy-start.83 = (pred[12]{0:T(512)(128)(4,1)S(1)}, pred[12]{0:T(512)(128)(4,1)}, u32[]{:S(2)}) copy-start(pred[12]{0:T(512)(128)(4,1)} %get-tuple-element.802) | copy-start | bytes 40
  153.4 28.1 %copy-start.36 = (pred[12]{0:T(512)(128)(4,1)S(1)}, pred[12]{0:T(512)(128)(4,1)}, u32[]{:S(2)}) copy-start(pred[12]{0:T(512)(128)(4,1)} %get-tuple-element.801) | copy-start | bytes 40
  153.4 28.8 %copy-start.74 = (pred[12]{0:T(512)(128)(4,1)S(1)}, pred[12]{0:T(512)(128)(4,1)}, u32[]{:S(2)}) copy-start(pred[12]{0:T(512)(128)(4,1)} %get-tuple-element.800) | copy-start | bytes 40
  153.4 29.5 %copy-start.34 = (pred[12]{0:T(512)(128)(4,1)S(1)}, pred[12]{0:T(512)(128)(4,1)}, u32[]{:S(2)}) copy-start(pred[12]{0:T(512)(128)(4,1)} %get-tuple-element.799) | copy-start | bytes 40
  153.4 30.2 %copy-start.72 = (pred[12]{0:T(512)(128)(4,1)S(1)}, pred[12]{0:T(512)(128)(4,1)}, u32[]{:S(2)}) copy-start(pred[12]{0:T(512)(128)(4,1)} %get-tuple-element.798) | copy-start | bytes 40
  153.4 30.8 %copy-start.18 = (bf16[27,96,96]{2,1,0:T(8,128)(2,1)S(1)}, bf16[27,96,96]{2,1,0:T(8,128)(2,1)}, u32[]{:S(2)}) copy-start(bf16[27,96,96]{2,1,0:T(8,128)(2,1)} %param.141) | copy-start | bytes 1492996
  305.3 55.4 %copy-start.23 = (bf16[8,192,512]{2,1,0:T(8,128)(2,1)S(1)}, bf16[8,192,512]{2,1,0:T(8,128)(2,1)}, u32[]{:S(2)}) copy-start(bf16[8,192,512]{2,1,0:T(8,128)(2,1)} %param.143) | copy-start | bytes 4718596
  363.9 25.4 %all-to-all-start.1 = ((bf16[8,192,512]{2,1,0:T(8,128)(2,1)}), bf16[8,192,512]{2,1,0:T(8,128)(2,1)}, u32[]{:S(2)}, u32[]{:S(2)}) async-start(bf16[8,192,512]{2,1,0:T(8,128)(2,1)} %get-tuple-element.762), calls=%async_computation.1 | async-start | bytes 3145728 | tf_op jit(solution)/shard_map/all_to_all | solution.py:183
  368.2 231.0 %all-reduce.5.cloned.1.call-start = ((), (), s32[]{:S(2)}) async-start(), calls=%async_computation.2 | async-start | bytes 4227072 | tf_op jit(solution)/shard_map/psum | solution.py:204
  411.5 9.5 %copy-start.3 = (bf16[12,96,10,10,10]{1,0,4,3,2:T(8,128)(2,1)S(1)}, bf16[12,96,10,10,10]{1,0,4,3,2:T(8,128)(2,1)}, u32[]{:S(2)}) copy-start(bf16[12,96,10,10,10]{1,0,4,3,2:T(8,128)(2,1)} %constant_dynamic-update-slice_fusion.7) | copy-start | bytes 6912004
  411.5 41.6 %collective-permute-start.5 = (bf16[1,1,8,96,512]{4,3,2,1,0:T(8,128)(2,1)S(1)}, bf16[1,1,8,96,512]{4,3,2,1,0:T(8,128)(2,1)S(1)}, u32[]{:S(2)}, u32[]{:S(2)}) collective-permute-start(bf16[1,1,8,96,512]{4,3,2,1,0:T(8,128)(2,1)S(1)} %select_bitcast_fusion), channel_id=1, source_target_pairs={{8,0},{16,8},{24,16},{9,1},{17,9},{25,17},{10,2},{18,10},{26,18},{... | collective-permute-start | bytes 2359304 | tf_op jit(solution)/shard_map/ppermute | solution.py:17
  413.1 40.0 %collective-permute-start.4 = (bf16[1,1,8,96,512]{4,3,2,1,0:T(8,128)(2,1)S(1)}, bf16[1,1,8,96,512]{4,3,2,1,0:T(8,128)(2,1)S(1)}, u32[]{:S(2)}, u32[]{:S(2)}) collective-permute-start(bf16[1,1,8,96,512]{4,3,2,1,0:T(8,128)(2,1)S(1)} %select_bitcast_fusion), channel_id=1, source_target_pairs={{0,8},{8,16},{16,24},{1,9},{9,17},{17,25},{2,10},{10,18},{18,26},{... | collective-permute-start | bytes 2359304 | tf_op jit(solution)/shard_map/ppermute | solution.py:16
  453.0 9.3 %copy-start.16 = (bf16[1,1,8,96,512]{4,3,2,1,0:T(8,128)(2,1)}, bf16[1,1,8,96,512]{4,3,2,1,0:T(8,128)(2,1)S(1)}, u32[]{:S(2)}) copy-start(bf16[1,1,8,96,512]{4,3,2,1,0:T(8,128)(2,1)S(1)} %collective-permute-done.5) | copy-start | bytes 2359300
  453.1 9.3 %copy-start.17 = (bf16[1,1,8,96,512]{4,3,2,1,0:T(8,128)(2,1)}, bf16[1,1,8,96,512]{4,3,2,1,0:T(8,128)(2,1)S(1)}, u32[]{:S(2)}) copy-start(bf16[1,1,8,96,512]{4,3,2,1,0:T(8,128)(2,1)S(1)} %collective-permute-done.4) | copy-start | bytes 2359300
  454.8 146.7 %collective-permute-start.7 = (bf16[3,1,8,96,512]{4,3,2,1,0:T(8,128)(2,1)}, bf16[3,1,8,96,512]{4,3,2,1,0:T(8,128)(2,1)}, u32[]{:S(2)}, u32[]{:S(2)}) collective-permute-start(bf16[3,1,8,96,512]{4,3,2,1,0:T(8,128)(2,1)} %pad_maximum_fusion.3), channel_id=1, source_target_pairs={{1,0},{2,1},{3,2},{4,3},{5,4},{6,5},{7,6},{9,8},{10,9},{11,10},{12... | collective-permute-start | bytes 7077896 | tf_op jit(solution)/shard_map/ppermute | solution.py:17
  456.2 145.3 %collective-permute-start.6 = (bf16[3,1,8,96,512]{4,3,2,1,0:T(8,128)(2,1)}, bf16[3,1,8,96,512]{4,3,2,1,0:T(8,128)(2,1)}, u32[]{:S(2)}, u32[]{:S(2)}) collective-permute-start(bf16[3,1,8,96,512]{4,3,2,1,0:T(8,128)(2,1)} %pad_maximum_fusion.3), channel_id=1, source_target_pairs={{0,1},{1,2},{2,3},{3,4},{4,5},{5,6},{6,7},{8,9},{9,10},{10,11},{11... | collective-permute-start | bytes 7077896 | tf_op jit(solution)/shard_map/ppermute | solution.py:16
  607.8 12.1 %copy-start.97 = (bf16[85]{0:T(256)(128)(2,1)S(1)}, bf16[85]{0:T(256)(128)(2,1)}, u32[]{:S(2)}) copy-start(bf16[85]{0:T(256)(128)(2,1)} %pad.231.clone) | copy-start | bytes 514
  687.4 68.5 %copy-start.4 = (bf16[12,96,10,10,10]{1,0,4,3,2:T(8,128)(2,1)}, bf16[12,96,10,10,10]{1,0,4,3,2:T(8,128)(2,1)S(1)}, u32[]{:S(2)}) copy-start(bf16[12,96,10,10,10]{1,0,4,3,2:T(8,128)(2,1)S(1)} %constant_dynamic-update-slice_fusion) | copy-start | bytes 6912004
  758.6 40.2 %copy-start.1 = (bf16[8,192,96]{2,1,0:T(8,128)(2,1)S(1)}, bf16[8,192,96]{2,1,0:T(8,128)(2,1)}, u32[]{:S(2)}) copy-start(bf16[8,192,96]{2,1,0:T(8,128)(2,1)} %param.142) | copy-start | bytes 884740
  (48 other events, 218.5 us)
Sparse Core Ops, SparseCore 0:
  466.7 132.4 all-reduce.4
where the time goes:
time: 815 us; the launch traced here: 806 us
  matrix products  260 us (32%)
  local copies, waits for them, and re-layouts  183 us (22%)
  waiting for transfers between devices  149 us (18%)
  other arithmetic  112 us (14%)
  blocking collectives  55.4 us (7%)
  starting transfers between devices  30.3 us (4%)
  between operations  16.4 us (2%)
    psum x1, waiting for transfers between devices, on_device(): grad_sub, grad_down = lax.psum((sub_local, down_local), ('gx', 'yz'))  133 us
    dot_general x27, matrix products, conv_forward(): jnp.einsum('oi,bixyz->boxyz', weights[offset], window, preferred_element_...  110 us
    dot_general x27, matrix products, conv_transpose(): jnp.einsum('oi,boxyz->bixyz', weights[offset], window, preferred_element_...  106 us
    gather x54, local copies, waits for them, and re-layouts, pad_bricks(): picked = jnp.take(facing, neighbour_ids[:, offset], axis=0)  63.4 us
    all_to_all x1, blocking collectives, on_device(): lax.all_to_all(outgoing, 'yz', split_axis=0, concat_axis=0, tiled=True)  55.4 us
    dot_general x27, matrix products, conv_weights(): jnp.einsum('boxyz,bixyz->oi', grads, window, preferred_element_type=jnp.f...  39.1 us
    scatter x52, other arithmetic, pad_bricks(): padded = padded.at[:, :, spans[0][1], spans[1][1], spans[2][1]].set(picked)  35.7 us
    another operation x50, local copies, waits for them, and re-layouts, pad_bricks(): picked = jnp.take(facing, neighbour_ids[:, offset], axis=0)  33.3 us
  transfers between devices with their start and end apart: 10, of which 2 were waited for; matrix products, arithmetic and copies ran while one was open for 10% of the time, Pallas kernels for 0%

commit v1 on v0

--- a/solution.py
+++ b/solution.py
@@ -4,6 +4,22 @@
 from jax.sharding import PartitionSpec as P
 
 EDGE = 8
+
+
+def pairwise_exchange(array, axis, split, join):
+    ways, here = (lax.axis_size(axis), lax.axis_index(axis))
+    width = array.shape[split] // ways
+    shape = list(array.shape)
+    shape[split] = width
+    height = shape[join]
+    shape[join] = height * ways
+    full = jnp.zeros(shape, array.dtype)
+    for mask in range(ways):
+        part = lax.dynamic_slice_in_dim(array, (here ^ mask) * width, width, axis=split)
+        if mask:
+            part = lax.ppermute(part, axis, [(d, d ^ mask) for d in range(ways)])
+        full = lax.dynamic_update_slice_in_dim(full, part, (here ^ mask) * height, axis=join)
+    return full
 
 
 def padded_2(x, sides, width):
@@ -177,7 +193,7 @@
         ),
         half_edge,
     )
-    coarse_pre = lax.all_to_all(outgoing, "yz", split_axis=0, concat_axis=0, tiled=True)
+    coarse_pre = pairwise_exchange(outgoing, "yz", 0, 0)
     grad_coarse = activate_coarse(coarse_pre, cotangent)
     returned = split_block(
         lax.all_to_all(grad_coarse, "yz", split_axis=0, concat_axis=0, tiled=True), half_edge

time: 815 us -> 843 us (1.034)
  blocking collectives: 55.4 us -> 0 us
  starting transfers between devices: 30.3 us -> 67.5 us
  waiting for transfers between devices: 149 us -> 183 us
  local copies, waits for them, and re-layouts: 183 us -> 194 us
    all_to_all x1 -> x0, blocking collectives: 55.4 us -> none  [on_device(): lax.all_to_all(outgoing, 'yz', split_axis=0, concat_axis=0, tiled=True)]
    ppermute x0 -> x7, starting transfers between devices: none -> 37.2 us  [pairwise_exchange(): part = lax.ppermute(part, axis, [(d, d ^ mask) for d in range(ways)])]
    ppermute x0 -> x7, waiting for transfers between devices: none -> 33.5 us  [pairwise_exchange(): part = lax.ppermute(part, axis, [(d, d ^ mask) for d in range(ways)])]
  transfers between devices with their start and end apart: 10 -> 17, of which waited for: 2 -> 5; matrix products, arithmetic and copies ran while one was open for 10% -> 11% of each run, Pallas kernels for 0% -> 0%
where the time goes in v1:
time: 843 us; the launch traced here: 834 us
  matrix products  260 us (31%)
  local copies, waits for them, and re-layouts  194 us (23%)
  waiting for transfers between devices  183 us (22%)
  other arithmetic  113 us (13%)
  starting transfers between devices  67.5 us (8%)
  between operations  16.5 us (2%)
    psum x1, waiting for transfers between devices, on_device(): grad_sub, grad_down = lax.psum((sub_local, down_local), ('gx', 'yz'))  133 us
    dot_general x27, matrix products, conv_forward(): jnp.einsum('oi,bixyz->boxyz', weights[offset], window, preferred_element_...  110 us
    dot_general x27, matrix products, conv_transpose(): jnp.einsum('oi,boxyz->bixyz', weights[offset], window, preferred_element_...  106 us
    gather x54, local copies, waits for them, and re-layouts, pad_bricks(): picked = jnp.take(facing, neighbour_ids[:, offset], axis=0)  63.4 us
    dot_general x27, matrix products, conv_weights(): jnp.einsum('boxyz,bixyz->oi', grads, window, preferred_element_type=jnp.f...  39.1 us
    ppermute x7, starting transfers between devices, pairwise_exchange(): part = lax.ppermute(part, axis, [(d, d ^ mask) for d in range(ways)])  37.2 us
    scatter x52, other arithmetic, pad_bricks(): padded = padded.at[:, :, spans[0][1], spans[1][1], spans[2][1]].set(picked)  35.6 us
    ppermute x7, waiting for transfers between devices, pairwise_exchange(): part = lax.ppermute(part, axis, [(d, d ^ mask) for d in range(ways)])  33.5 us
  transfers between devices with their start and end apart: 17, of which 5 were waited for; matrix products, arithmetic and copies ran while one was open for 11% of the time, Pallas kernels for 0%

profile of v1, /device:TPU:0, one launch (start us, length us, event | category | flops | bytes accessed | tf_op | source)
XLA Modules:
  0.0 834.1 jit_solution(11515094739823182406)
XLA Ops:
  13.5 6.5 collective-permute-start
  38.2 3.1 pad_maximum_fusion.2
  42.6 4.5 collective-permute-start.2
  47.8 3.3 copy.312
  66.3 6.2 pad_maximum_fusion
  72.6 12.1 %copy.313 = bf16[3,3,8,96,512]{3,2,1,0,4:T(8,128)(2,1)} copy(bf16[3,3,8,96,512]{4,3,2,1,0:T(8,128)(2,1)} %pad_maximum_fusion) | data formatting | bytes 14155776 | tf_op jit(solution)/shard_map/concatenate | solution.py:34
  84.6 8.6 %maximum_maximum_fusion = bf16[85,96,8,8,8]{1,0,4,3,2:T(8,128)(2,1)S(1)} fusion(bf16[72,96,8,8,8]{1,0,4,3,2:T(8,128)(2,1)} %bitcast.1018, bf16[12,96,8,8,8]{1,0,4,3,2:T(8,128)(2,1)S(1)} %bitcast.1025, bf16[85]{0:T(256)(128)(2,1)S(1)} %copy-done.96), kind=kLoop, calls=%fused_computation.57 | loop fusion | flops 25067520 | bytes 16613546 | tf_op jit(solution)/shard_map/concatenate | solution.py:155
  94.9 6.4 copy.332
  144.0 5.1 gather_fusion.15
  170.5 4.3 fusion.66
  184.2 4.5 fusion.281
  188.7 2.7 fusion.285
  194.1 2.8 fusion.293
  199.6 2.7 fusion.301
  202.3 2.7 fusion.305
  205.1 2.8 fusion.309
  207.9 3.1 fusion.313
  216.3 2.8 fusion.325
  221.8 2.7 fusion.333
  227.1 2.8 fusion.341
  232.6 2.7 fusion.349
  235.4 2.7 fusion.353
  238.1 2.8 fusion.357
  243.6 2.7 fusion.365
  246.4 2.7 fusion.369
  249.1 2.8 fusion.373
  257.3 37.1 %multiply_convert_fusion.1 = (bf16[12,96,8,8,8]{1,0,4,3,2:T(8,128)(2,1)S(1)}, f32[12,96,8,8,8]{1,0,4,3,2:T(8,128)}) fusion(f32[12,8,8,8]{0,3,2,1:T(8,128)S(1)} %bitcast.1029, bf16[12,96,10,10,10]{1,0,4,3,2:T(8,128)(2,1)} %constant_dynamic-update-slice_fusion.15, bf16[27,96,96]{2,1,0:T(8,128)(2,1)} %param.141, f32[12,8,8,8,96]{4,0,3,2,1:T(8,128)} %fusion.281, ...), kind=kOutput, calls=%fused_computation.88 | convolution fusion | flops 132120576 | bytes 116736000 | tf_op jit(solution)/shard_map/oi,bixyz->boxyz/dot_general | solution.py:80
  302.3 5.4 constant_dynamic-slice_fusion
  307.7 33.0 %collective-permute-start.9 = (bf16[1,192,512]{1,0,2:T(2,128)(2,1)}, bf16[1,192,512]{1,0,2:T(2,128)(2,1)}, u32[]{:S(2)}, u32[]{:S(2)}) collective-permute-start(bf16[1,192,512]{1,0,2:T(2,128)(2,1)} %get-tuple-element.763), channel_id=1, source_target_pairs={{0,6},{1,7},{2,4},{3,5},{4,2},{5,3},{6,0},{7,1},{8,14},{9,15},{10,... | collective-permute-start | bytes 589832 | tf_op jit(solution)/shard_map/ppermute | solution.py:20
  344.9 9.0 %collective-permute-done.9 = bf16[1,192,512]{1,0,2:T(2,128)(2,1)} collective-permute-done((bf16[1,192,512]{1,0,2:T(2,128)(2,1)}, bf16[1,192,512]{1,0,2:T(2,128)(2,1)}, u32[]{:S(2)}, u32[]{:S(2)}) %collective-permute-start.9) | collective-permute-done | bytes 196640 | tf_op jit(solution)/shard_map/ppermute | solution.py:20
  355.1 10.1 %collective-permute-done.7 = bf16[1,192,512]{1,0,2:T(2,128)(2,1)} collective-permute-done((bf16[1,192,512]{1,0,2:T(2,128)(2,1)}, bf16[1,192,512]{1,0,2:T(2,128)(2,1)}, u32[]{:S(2)}, u32[]{:S(2)}) %collective-permute-start.7) | collective-permute-done | bytes 196640 | tf_op jit(solution)/shard_map/ppermute | solution.py:20
  369.5 14.4 %collective-permute-done.6 = bf16[1,192,512]{1,0,2:T(2,128)(2,1)} collective-permute-done((bf16[1,192,512]{1,0,2:T(2,128)(2,1)}, bf16[1,192,512]{1,0,2:T(2,128)(2,1)}, u32[]{:S(2)}, u32[]{:S(2)}) %collective-permute-start.6) | collective-permute-done | bytes 196640 | tf_op jit(solution)/shard_map/ppermute | solution.py:20
  386.8 4.6 fusion.10
  391.5 4.3 all-to-all-start
  395.8 4.4 copy.409
  400.3 16.9 %all-to-all-done = bf16[8,192,512]{2,1,0:T(8,128)(2,1)} async-done(((bf16[8,192,512]{2,1,0:T(8,128)(2,1)}), bf16[8,192,512]{2,1,0:T(8,128)(2,1)}, u32[]{:S(2)}, u32[]{:S(2)}) %all-to-all-start) | async-done | bytes 1572896 | tf_op jit(solution)/shard_map/all_to_all | solution.py:199
  417.1 3.2 copy.364
  420.4 3.5 copy.365
  423.8 3.6 reshape.2536
  435.5 2.9 gather_fusion.29
  441.2 5.0 collective-permute-start.11
  446.2 3.0 fusion.72
  484.4 4.5 collective-permute-start.13
  494.7 132.6 %all-reduce.5.cloned.1.call-done = (f32[27,96,96]{2,1,0:T(8,128)}, f32[8,192,96]{1,0,2:T(8,128)}) async-done(((f32[27,96,96]{2,1,0:T(8,128)}, f32[8,192,96]{1,0,2:T(8,128)}), (f32[27,96,96]{2,1,0:T(8,128)}, f32[8,192,96]{1,0,2:T(8,128)})) %all-reduce.5.cloned.1.call-update) | async-done | bytes 1585168 | tf_op jit(solution)/shard_map/psum | solution.py:220
  629.6 6.2 pad_maximum_fusion.1
  635.9 12.1 %copy.474 = bf16[3,3,8,96,512]{3,2,1,0,4:T(8,128)(2,1)} copy(bf16[3,3,8,96,512]{4,3,2,1,0:T(8,128)(2,1)} %pad_maximum_fusion.1) | data formatting | bytes 14155776 | tf_op jit(solution)/shard_map/concatenate | solution.py:155
  647.9 8.6 %maximum_maximum_fusion.1 = bf16[85,96,8,8,8]{1,0,4,3,2:T(8,128)(2,1)S(1)} fusion(bf16[72,96,8,8,8]{1,0,4,3,2:T(8,128)(2,1)} %bitcast.1017, bf16[12,96,8,8,8]{1,0,4,3,2:T(8,128)(2,1)S(1)} %multiply_convert_fusion, bf16[85]{0:T(256)(128)(2,1)S(1)} %copy-done.97), kind=kLoop, calls=%fused_computation.58 | loop fusion | flops 25067520 | bytes 16613546 | tf_op jit(solution)/shard_map/concatenate | solution.py:155
  662.6 6.3 copy.389
  694.4 5.1 gather_fusion.43
  699.6 2.8 copy.395
  704.4 2.8 copy.383
  715.5 3.1 fusion.279
  721.3 2.8 fusion.287
  726.7 2.7 fusion.295
  732.2 2.8 fusion.303
  737.6 3.0 fusion.311
  743.2 2.8 fusion.319
  754.0 2.8 fusion.335
  759.4 2.7 fusion.343
  764.9 2.8 fusion.351
  770.4 2.7 fusion.359
  775.8 2.8 fusion.367
  781.3 2.7 fusion.375
  786.7 35.1 %fusion.1 = bf16[12,96,8,8,8]{1,0,4,3,2:T(8,128)(2,1)S(1)} fusion(f32[12,8,8,8,96]{4,0,3,2,1:T(8,128)} %fusion.279, f32[12,8,8,8,96]{4,0,3,2,1:T(8,128)} %fusion.283, f32[12,8,8,8,96]{4,0,3,2,1:T(8,128)} %fusion.287, f32[12,8,8,8,96]{4,0,3,2,1:T(8,128)} %fusion.291, f32[12,8,8,8,96]{4,0,3,2,1:T(8,128)} %fusion.295, f32[12,8,8,8,96]{4,0,3,2,1:T(8,128)} %fusion.299, ...), kind=kOutput, calls=%fused_computation.66 | convolution fusion | flops 129761280 | bytes 114376704 | tf_op jit(solution)/shard_map/oi,boxyz->bixyz/dot_general | solution.py:98
  (537 shorter events, 301.0 us)
Async XLA Ops:
  7.2 289.3 %copy-start = (bf16[8,192,96]{2,1,0:T(8,128)(2,1)S(1)}, bf16[8,192,96]{2,1,0:T(8,128)(2,1)}, u32[]{:S(2)}) copy-start(bf16[8,192,96]{2,1,0:T(8,128)(2,1)} %param.142) | copy-start | bytes 884740
  7.2 12.8 %copy-start.11 = (s32[12,27]{1,0:T(8,128)S(1)}, s32[12,27]{1,0:T(8,128)}, u32[]{:S(2)}) copy-start(s32[12,27]{1,0:T(8,128)} %param.137) | copy-start | bytes 3892
  7.2 13.6 %copy-start.95 = (s32[12,2]{0,1:T(2,128)S(1)}, s32[12,2]{0,1:T(2,128)}, u32[]{:S(2)}) copy-start(s32[12,2]{0,1:T(2,128)} %param.139) | copy-start | bytes 292
  7.2 14.9 %copy-start.5 = (s32[4]{0:T(128)S(1)}, s32[4]{0:T(128)}, u32[]{:S(2)}) copy-start(s32[4]{0:T(128)} %param.140) | copy-start | bytes 52
  7.9 33.4 %copy-start.98 = (pred[8]{0:T(512)(128)(4,1)}, pred[8]{0:T(512)(128)(4,1)S(1)}, u32[]{:S(2)}) copy-start(pred[8]{0:T(512)(128)(4,1)S(1)} %compare_and_fusion.27) | copy-start | bytes 28
  8.6 32.7 %copy-start.33 = (s32[1024]{0:T(1024)}, s32[1024]{0:T(1024)S(1)}, u32[]{:S(2)}) copy-start(s32[1024]{0:T(1024)S(1)} %pad_clamp_fusion.28) | copy-start | bytes 12292
  11.4 29.9 %copy-start.8 = (bf16[12,96,512]{2,1,0:T(8,128)(2,1)}, bf16[12,96,512]{2,1,0:T(8,128)(2,1)S(1)}, u32[]{:S(2)}) copy-start(bf16[12,96,512]{2,1,0:T(8,128)(2,1)S(1)} %broadcast_multiply_fusion) | copy-start | bytes 3538948
  12.2 26.0 %collective-permute-start.1 = (bf16[1,1,8,96,512]{4,3,2,1,0:T(8,128)(2,1)S(1)}, bf16[1,1,8,96,512]{4,3,2,1,0:T(8,128)(2,1)S(1)}, u32[]{:S(2)}, u32[]{:S(2)}) collective-permute-start(bf16[1,1,8,96,512]{4,3,2,1,0:T(8,128)(2,1)S(1)} %select_bitcast_fusion.1), channel_id=1, source_target_pairs={{8,0},{16,8},{24,16},{9,1},{17,9},{25,17},{10,2},{18,10},{26,18},{... | collective-permute-start | bytes 2359304 | tf_op jit(solution)/shard_map/ppermute | solution.py:33
  13.5 24.7 %collective-permute-start = (bf16[1,1,8,96,512]{4,3,2,1,0:T(8,128)(2,1)S(1)}, bf16[1,1,8,96,512]{4,3,2,1,0:T(8,128)(2,1)}, u32[]{:S(2)}, u32[]{:S(2)}) collective-permute-start(bf16[1,1,8,96,512]{4,3,2,1,0:T(8,128)(2,1)S(1)} %select_bitcast_fusion.1), channel_id=1, source_target_pairs={{0,8},{8,16},{16,24},{1,9},{9,17},{17,25},{2,10},{10,18},{18,26},{... | collective-permute-start | bytes 2359304 | tf_op jit(solution)/shard_map/ppermute | solution.py:32
  20.3 27.4 %copy-start.52 = (s32[12]{0:T(128)}, s32[12]{0:T(128)S(1)}, u32[]{:S(2)}) copy-start(s32[12]{0:T(128)S(1)} %get-tuple-element.700) | copy-start | bytes 148
  20.3 27.4 %copy-start.70 = (s32[12]{0:T(128)}, s32[12]{0:T(128)S(1)}, u32[]{:S(2)}) copy-start(s32[12]{0:T(128)S(1)} %get-tuple-element.699) | copy-start | bytes 148
  20.9 26.8 %copy-start.53 = (s32[12]{0:T(128)}, s32[12]{0:T(128)S(1)}, u32[]{:S(2)}) copy-start(s32[12]{0:T(128)S(1)} %get-tuple-element.698) | copy-start | bytes 148
  20.9 26.8 %copy-start.54 = (s32[12]{0:T(128)}, s32[12]{0:T(128)S(1)}, u32[]{:S(2)}) copy-start(s32[12]{0:T(128)S(1)} %get-tuple-element.696) | copy-start | bytes 148
  20.9 26.8 %copy-start.55 = (s32[12]{0:T(128)}, s32[12]{0:T(128)S(1)}, u32[]{:S(2)}) copy-start(s32[12]{0:T(128)S(1)} %get-tuple-element.697) | copy-start | bytes 148
  20.9 26.8 %copy-start.56 = (s32[12]{0:T(128)}, s32[12]{0:T(128)S(1)}, u32[]{:S(2)}) copy-start(s32[12]{0:T(128)S(1)} %get-tuple-element.694) | copy-start | bytes 148
  20.9 26.8 %copy-start.57 = (s32[12]{0:T(128)}, s32[12]{0:T(128)S(1)}, u32[]{:S(2)}) copy-start(s32[12]{0:T(128)S(1)} %get-tuple-element.695) | copy-start | bytes 148
  20.9 26.8 %copy-start.58 = (s32[12]{0:T(128)}, s32[12]{0:T(128)S(1)}, u32[]{:S(2)}) copy-start(s32[12]{0:T(128)S(1)} %get-tuple-element.692) | copy-start | bytes 148
  20.9 26.8 %copy-start.59 = (s32[12]{0:T(128)}, s32[12]{0:T(128)S(1)}, u32[]{:S(2)}) copy-start(s32[12]{0:T(128)S(1)} %get-tuple-element.693) | copy-start | bytes 148
  20.9 26.8 %copy-start.60 = (s32[12]{0:T(128)}, s32[12]{0:T(128)S(1)}, u32[]{:S(2)}) copy-start(s32[12]{0:T(128)S(1)} %get-tuple-element.690) | copy-start | bytes 148
  20.9 26.8 %copy-start.61 = (s32[12]{0:T(128)}, s32[12]{0:T(128)S(1)}, u32[]{:S(2)}) copy-start(s32[12]{0:T(128)S(1)} %get-tuple-element.691) | copy-start | bytes 148
  21.0 26.8 %copy-start.62 = (s32[12]{0:T(128)}, s32[12]{0:T(128)S(1)}, u32[]{:S(2)}) copy-start(s32[12]{0:T(128)S(1)} %get-tuple-element.688) | copy-start | bytes 148
  21.0 26.8 %copy-start.63 = (s32[12]{0:T(128)}, s32[12]{0:T(128)S(1)}, u32[]{:S(2)}) copy-start(s32[12]{0:T(128)S(1)} %get-tuple-element.689) | copy-start | bytes 148
  21.0 26.8 %copy-start.66 = (s32[12]{0:T(128)}, s32[12]{0:T(128)S(1)}, u32[]{:S(2)}) copy-start(s32[12]{0:T(128)S(1)} %get-tuple-element.684) | copy-start | bytes 148
  21.0 26.8 %copy-start.67 = (s32[12]{0:T(128)}, s32[12]{0:T(128)S(1)}, u32[]{:S(2)}) copy-start(s32[12]{0:T(128)S(1)} %get-tuple-element.685) | copy-start | bytes 148
  21.0 26.8 %copy-start.68 = (s32[12]{0:T(128)}, s32[12]{0:T(128)S(1)}, u32[]{:S(2)}) copy-start(s32[12]{0:T(128)S(1)} %get-tuple-element.682) | copy-start | bytes 148
  21.0 26.8 %copy-start.69 = (s32[12]{0:T(128)}, s32[12]{0:T(128)S(1)}, u32[]{:S(2)}) copy-start(s32[12]{0:T(128)S(1)} %get-tuple-element.683) | copy-start | bytes 148
  21.0 26.8 %copy-start.71 = (s32[12]{0:T(128)}, s32[12]{0:T(128)S(1)}, u32[]{:S(2)}) copy-start(s32[12]{0:T(128)S(1)} %get-tuple-element.681) | copy-start | bytes 148
  25.1 87.7 %copy-start.29 = (s32[1024]{0:T(1024)}, s32[1024]{0:T(1024)S(1)}, u32[]{:S(2)}) copy-start(s32[1024]{0:T(1024)S(1)} %pad_clamp_fusion.27) | copy-start | bytes 12292
  29.9 88.1 %copy-start.30 = (s32[1024]{0:T(1024)}, s32[1024]{0:T(1024)S(1)}, u32[]{:S(2)}) copy-start(s32[1024]{0:T(1024)S(1)} %pad_clamp_fusion.9) | copy-start | bytes 12292
  30.0 87.5 %copy-start.31 = (s32[1024]{0:T(1024)}, s32[1024]{0:T(1024)S(1)}, u32[]{:S(2)}) copy-start(s32[1024]{0:T(1024)S(1)} %pad_clamp_fusion.7) | copy-start | bytes 12292
  30.6 86.2 %copy-start.32 = (s32[1024]{0:T(1024)}, s32[1024]{0:T(1024)S(1)}, u32[]{:S(2)}) copy-start(s32[1024]{0:T(1024)S(1)} %pad_clamp_fusion.3) | copy-start | bytes 12292
  41.3 25.0 %collective-permute-start.3 = (bf16[3,1,8,96,512]{4,3,2,1,0:T(8,128)(2,1)}, bf16[3,1,8,96,512]{4,3,2,1,0:T(8,128)(2,1)}, u32[]{:S(2)}, u32[]{:S(2)}) collective-permute-start(bf16[3,1,8,96,512]{4,3,2,1,0:T(8,128)(2,1)} %pad_maximum_fusion.2), channel_id=1, source_target_pairs={{1,0},{2,1},{3,2},{4,3},{5,4},{6,5},{7,6},{9,8},{10,9},{11,10},{12... | collective-permute-start | bytes 7077896 | tf_op jit(solution)/shard_map/ppermute | solution.py:33
  42.6 23.7 %collective-permute-start.2 = (bf16[3,1,8,96,512]{4,3,2,1,0:T(8,128)(2,1)}, bf16[3,1,8,96,512]{4,3,2,1,0:T(8,128)(2,1)}, u32[]{:S(2)}, u32[]{:S(2)}) collective-permute-start(bf16[3,1,8,96,512]{4,3,2,1,0:T(8,128)(2,1)} %pad_maximum_fusion.2), channel_id=1, source_target_pairs={{0,1},{1,2},{2,3},{3,4},{4,5},{5,6},{6,7},{8,9},{9,10},{10,11},{11... | collective-permute-start | bytes 7077896 | tf_op jit(solution)/shard_map/ppermute | solution.py:32
  52.0 205.3 %copy-start.12 = (f32[12,512]{0,1:T(8,128)}, f32[12,512]{0,1:T(8,128)S(1)}, u32[]{:S(2)}) copy-start(f32[12,512]{0,1:T(8,128)S(1)} %copy.471) | copy-start | bytes 73732
  153.3 21.5 %copy-start.88 = (pred[12]{0:T(512)(128)(4,1)S(1)}, pred[12]{0:T(512)(128)(4,1)}, u32[]{:S(2)}) copy-start(pred[12]{0:T(512)(128)(4,1)} %get-tuple-element.818) | copy-start | bytes 40
  153.3 22.4 %copy-start.15 = (bf16[12,96,8]{1,2,0:T(8,128)(2,1)S(1)}, bf16[12,96,8]{1,2,0:T(8,128)(2,1)}, u32[]{:S(2)}) copy-start(bf16[12,96,8]{1,2,0:T(8,128)(2,1)} %gather_fusion.17) | copy-start | bytes 55300
  153.3 22.4 %copy-start.47 = (pred[12]{0:T(512)(128)(4,1)S(1)}, pred[12]{0:T(512)(128)(4,1)}, u32[]{:S(2)}) copy-start(pred[12]{0:T(512)(128)(4,1)} %get-tuple-element.817) | copy-start | bytes 40
  153.3 23.0 %copy-start.86 = (pred[12]{0:T(512)(128)(4,1)S(1)}, pred[12]{0:T(512)(128)(4,1)}, u32[]{:S(2)}) copy-start(pred[12]{0:T(512)(128)(4,1)} %get-tuple-element.816) | copy-start | bytes 40
  153.3 23.9 %copy-start.45 = (pred[12]{0:T(512)(128)(4,1)S(1)}, pred[12]{0:T(512)(128)(4,1)}, u32[]{:S(2)}) copy-start(pred[12]{0:T(512)(128)(4,1)} %get-tuple-element.815) | copy-start | bytes 40
  153.3 24.6 %copy-start.80 = (pred[12]{0:T(512)(128)(4,1)S(1)}, pred[12]{0:T(512)(128)(4,1)}, u32[]{:S(2)}) copy-start(pred[12]{0:T(512)(128)(4,1)} %get-tuple-element.814) | copy-start | bytes 40
  153.3 25.2 %copy-start.43 = (pred[12]{0:T(512)(128)(4,1)S(1)}, pred[12]{0:T(512)(128)(4,1)}, u32[]{:S(2)}) copy-start(pred[12]{0:T(512)(128)(4,1)} %get-tuple-element.813) | copy-start | bytes 40
  153.4 25.9 %copy-start.78 = (pred[12]{0:T(512)(128)(4,1)S(1)}, pred[12]{0:T(512)(128)(4,1)}, u32[]{:S(2)}) copy-start(pred[12]{0:T(512)(128)(4,1)} %get-tuple-element.812) | copy-start | bytes 40
  153.4 26.5 %copy-start.41 = (pred[12]{0:T(512)(128)(4,1)S(1)}, pred[12]{0:T(512)(128)(4,1)}, u32[]{:S(2)}) copy-start(pred[12]{0:T(512)(128)(4,1)} %get-tuple-element.811) | copy-start | bytes 40
  153.4 27.2 %copy-start.84 = (pred[12]{0:T(512)(128)(4,1)S(1)}, pred[12]{0:T(512)(128)(4,1)}, u32[]{:S(2)}) copy-start(pred[12]{0:T(512)(128)(4,1)} %get-tuple-element.810) | copy-start | bytes 40
  153.4 28.1 %copy-start.39 = (pred[12]{0:T(512)(128)(4,1)S(1)}, pred[12]{0:T(512)(128)(4,1)}, u32[]{:S(2)}) copy-start(pred[12]{0:T(512)(128)(4,1)} %get-tuple-element.809) | copy-start | bytes 40
  153.4 28.8 %copy-start.76 = (pred[12]{0:T(512)(128)(4,1)S(1)}, pred[12]{0:T(512)(128)(4,1)}, u32[]{:S(2)}) copy-start(pred[12]{0:T(512)(128)(4,1)} %get-tuple-element.808) | copy-start | bytes 40
  153.4 29.4 %copy-start.37 = (pred[12]{0:T(512)(128)(4,1)S(1)}, pred[12]{0:T(512)(128)(4,1)}, u32[]{:S(2)}) copy-start(pred[12]{0:T(512)(128)(4,1)} %get-tuple-element.807) | copy-start | bytes 40
  153.4 30.1 %copy-start.74 = (pred[12]{0:T(512)(128)(4,1)S(1)}, pred[12]{0:T(512)(128)(4,1)}, u32[]{:S(2)}) copy-start(pred[12]{0:T(512)(128)(4,1)} %get-tuple-element.806) | copy-start | bytes 40
  153.4 30.7 %copy-start.19 = (bf16[27,96,96]{2,1,0:T(8,128)(2,1)S(1)}, bf16[27,96,96]{2,1,0:T(8,128)(2,1)}, u32[]{:S(2)}) copy-start(bf16[27,96,96]{2,1,0:T(8,128)(2,1)} %param.141) | copy-start | bytes 1492996
  307.7 46.2 %collective-permute-start.9 = (bf16[1,192,512]{1,0,2:T(2,128)(2,1)}, bf16[1,192,512]{1,0,2:T(2,128)(2,1)}, u32[]{:S(2)}, u32[]{:S(2)}) collective-permute-start(bf16[1,192,512]{1,0,2:T(2,128)(2,1)} %get-tuple-element.763), channel_id=1, source_target_pairs={{0,6},{1,7},{2,4},{3,5},{4,2},{5,3},{6,0},{7,1},{8,14},{9,15},{10,... | collective-permute-start | bytes 589832 | tf_op jit(solution)/shard_map/ppermute | solution.py:20
  340.7 24.5 %collective-permute-start.7 = (bf16[1,192,512]{1,0,2:T(2,128)(2,1)}, bf16[1,192,512]{1,0,2:T(2,128)(2,1)}, u32[]{:S(2)}, u32[]{:S(2)}) collective-permute-start(bf16[1,192,512]{1,0,2:T(2,128)(2,1)} %get-tuple-element.765), channel_id=1, source_target_pairs={{0,4},{1,5},{2,6},{3,7},{4,0},{5,1},{6,2},{7,3},{8,12},{9,13},{10,... | collective-permute-start | bytes 589832 | tf_op jit(solution)/shard_map/ppermute | solution.py:20
  340.7 26.2 %collective-permute-start.5 = (bf16[1,192,512]{1,0,2:T(2,128)(2,1)}, bf16[1,192,512]{1,0,2:T(2,128)(2,1)}, u32[]{:S(2)}, u32[]{:S(2)}) collective-permute-start(bf16[1,192,512]{1,0,2:T(2,128)(2,1)} %get-tuple-element.767), channel_id=1, source_target_pairs={{0,2},{1,3},{2,0},{3,1},{4,6},{5,7},{6,4},{7,5},{8,10},{9,11},{10,... | collective-permute-start | bytes 589832 | tf_op jit(solution)/shard_map/ppermute | solution.py:20
  341.9 26.3 %collective-permute-start.4 = (bf16[1,192,512]{1,0,2:T(2,128)(2,1)}, bf16[1,192,512]{1,0,2:T(2,128)(2,1)}, u32[]{:S(2)}, u32[]{:S(2)}) collective-permute-start(bf16[1,192,512]{1,0,2:T(2,128)(2,1)} %get-tuple-element.768), channel_id=1, source_target_pairs={{0,1},{1,0},{2,3},{3,2},{4,5},{5,4},{6,7},{7,6},{8,9},{9,8},{10,11... | collective-permute-start | bytes 589832 | tf_op jit(solution)/shard_map/ppermute | solution.py:20
  342.2 44.2 %collective-permute-start.10 = (bf16[1,192,512]{1,0,2:T(2,128)(2,1)}, bf16[1,192,512]{1,0,2:T(2,128)(2,1)S(1)}, u32[]{:S(2)}, u32[]{:S(2)}) collective-permute-start(bf16[1,192,512]{1,0,2:T(2,128)(2,1)} %get-tuple-element.762), channel_id=1, source_target_pairs={{0,7},{1,6},{2,5},{3,4},{4,3},{5,2},{6,1},{7,0},{8,15},{9,14},{10,... | collective-permute-start | bytes 589832 | tf_op jit(solution)/shard_map/ppermute | solution.py:20
  353.9 31.2 %collective-permute-start.8 = (bf16[1,192,512]{1,0,2:T(2,128)(2,1)}, bf16[1,192,512]{1,0,2:T(2,128)(2,1)}, u32[]{:S(2)}, u32[]{:S(2)}) collective-permute-start(bf16[1,192,512]{1,0,2:T(2,128)(2,1)} %get-tuple-element.764), channel_id=1, source_target_pairs={{0,5},{1,4},{2,7},{3,6},{4,1},{5,0},{6,3},{7,2},{8,13},{9,12},{10,... | collective-permute-start | bytes 589832 | tf_op jit(solution)/shard_map/ppermute | solution.py:20
  365.2 18.6 %collective-permute-start.6 = (bf16[1,192,512]{1,0,2:T(2,128)(2,1)}, bf16[1,192,512]{1,0,2:T(2,128)(2,1)}, u32[]{:S(2)}, u32[]{:S(2)}) collective-permute-start(bf16[1,192,512]{1,0,2:T(2,128)(2,1)} %get-tuple-element.766), channel_id=1, source_target_pairs={{0,3},{1,2},{2,1},{3,0},{4,7},{5,6},{6,5},{7,4},{8,11},{9,10},{10,... | collective-permute-start | bytes 589832 | tf_op jit(solution)/shard_map/ppermute | solution.py:20
  391.5 25.7 %all-to-all-start = ((bf16[8,192,512]{2,1,0:T(8,128)(2,1)}), bf16[8,192,512]{2,1,0:T(8,128)(2,1)}, u32[]{:S(2)}, u32[]{:S(2)}) async-start(bf16[8,192,512]{2,1,0:T(8,128)(2,1)} %get-tuple-element.770), calls=%async_computation | async-start | bytes 3145728 | tf_op jit(solution)/shard_map/all_to_all | solution.py:199
  395.8 231.5 %all-reduce.5.cloned.1.call-start = ((), (), s32[]{:S(2)}) async-start(), calls=%async_computation.1 | async-start | bytes 4227072 | tf_op jit(solution)/shard_map/psum | solution.py:220
  439.6 41.6 %collective-permute-start.12 = (bf16[1,1,8,96,512]{4,3,2,1,0:T(8,128)(2,1)S(1)}, bf16[1,1,8,96,512]{4,3,2,1,0:T(8,128)(2,1)S(1)}, u32[]{:S(2)}, u32[]{:S(2)}) collective-permute-start(bf16[1,1,8,96,512]{4,3,2,1,0:T(8,128)(2,1)S(1)} %select_bitcast_fusion), channel_id=1, source_target_pairs={{8,0},{16,8},{24,16},{9,1},{17,9},{25,17},{10,2},{18,10},{26,18},{... | collective-permute-start | bytes 2359304 | tf_op jit(solution)/shard_map/ppermute | solution.py:33
  441.2 40.0 %collective-permute-start.11 = (bf16[1,1,8,96,512]{4,3,2,1,0:T(8,128)(2,1)S(1)}, bf16[1,1,8,96,512]{4,3,2,1,0:T(8,128)(2,1)S(1)}, u32[]{:S(2)}, u32[]{:S(2)}) collective-permute-start(bf16[1,1,8,96,512]{4,3,2,1,0:T(8,128)(2,1)S(1)} %select_bitcast_fusion), channel_id=1, source_target_pairs={{0,8},{8,16},{16,24},{1,9},{9,17},{17,25},{2,10},{10,18},{18,26},{... | collective-permute-start | bytes 2359304 | tf_op jit(solution)/shard_map/ppermute | solution.py:32
  482.9 146.7 %collective-permute-start.14 = (bf16[3,1,8,96,512]{4,3,2,1,0:T(8,128)(2,1)}, bf16[3,1,8,96,512]{4,3,2,1,0:T(8,128)(2,1)}, u32[]{:S(2)}, u32[]{:S(2)}) collective-permute-start(bf16[3,1,8,96,512]{4,3,2,1,0:T(8,128)(2,1)} %pad_maximum_fusion.3), channel_id=1, source_target_pairs={{1,0},{2,1},{3,2},{4,3},{5,4},{6,5},{7,6},{9,8},{10,9},{11,10},{12... | collective-permute-start | bytes 7077896 | tf_op jit(solution)/shard_map/ppermute | solution.py:33
  484.4 145.3 %collective-permute-start.13 = (bf16[3,1,8,96,512]{4,3,2,1,0:T(8,128)(2,1)}, bf16[3,1,8,96,512]{4,3,2,1,0:T(8,128)(2,1)}, u32[]{:S(2)}, u32[]{:S(2)}) collective-permute-start(bf16[3,1,8,96,512]{4,3,2,1,0:T(8,128)(2,1)} %pad_maximum_fusion.3), channel_id=1, source_target_pairs={{0,1},{1,2},{2,3},{3,4},{4,5},{5,6},{6,7},{8,9},{9,10},{10,11},{11... | collective-permute-start | bytes 7077896 | tf_op jit(solution)/shard_map/ppermute | solution.py:32
  715.5 68.6 %copy-start.4 = (bf16[12,96,10,10,10]{1,0,4,3,2:T(8,128)(2,1)}, bf16[12,96,10,10,10]{1,0,4,3,2:T(8,128)(2,1)S(1)}, u32[]{:S(2)}) copy-start(bf16[12,96,10,10,10]{1,0,4,3,2:T(8,128)(2,1)S(1)} %constant_dynamic-update-slice_fusion) | copy-start | bytes 6912004
  786.7 40.2 %copy-start.1 = (bf16[8,192,96]{2,1,0:T(8,128)(2,1)S(1)}, bf16[8,192,96]{2,1,0:T(8,128)(2,1)}, u32[]{:S(2)}) copy-start(bf16[8,192,96]{2,1,0:T(8,128)(2,1)} %param.142) | copy-start | bytes 884740
  (55 other events, 283.1 us)
Sparse Core Ops, SparseCore 0:
  494.8 132.4 all-reduce.4
